TPU v7x, 32 devices: a whole 2x2x4 slice. The times are simulated.
32 devices in a mesh: group: 2 (over y), expert: 4 (over x, core), dp: 4 (over z).
Axes of the slice: x: 2, y: 2, z: 4, core: 2. Of those that a mesh axis runs over, the one named last changes fastest.
Arguments:
- cotangent: bfloat16 [8192, 7168], P(('group', 'expert', 'dp')), parts along dimension 0, may hold values from -6 to 6
- expert_ids: int32 [8192, 8], P(('group', 'expert', 'dp')), parts along dimension 0, may hold values from 0 to 255, all different within a row; in each aligned block of 128 rows (0 to 127, 128 to 255, ...) at most 8 rows name the same one
- gate_values: float32 [8192, 8], P(('group', 'expert', 'dp')), parts along dimension 0, may hold values from 0.02 to 0.3
- hidden: bfloat16 [8, 4, 4, 2, 8, 1024], P(('group', 'expert'), 'dp'), parts along dimension 0, may hold values from -6 to 6
- down_weight: bfloat16 [4, 1024, 7168], P('expert', None, 'dp'), may hold values from -0.1875 to 0.1875
Outputs:
- fisher: float32 [8, 1024, 7168], P(('group', 'expert'), None, 'dp'), parts along dimension 0
- hidden_grad: bfloat16 [8, 4, 4, 2, 8, 1024], P(('group', 'expert'), 'dp'), parts along dimension 0
There are 2 independent parts, one for each index of `group`. A program takes and returns all parts, laid end to end along the dimension named above; an argument that names none is the same for every part. Nothing has to cross between parts.
Inputs may be any that keep to these rules, and one draw needn't show every extreme that they name: `expert_ids`: each token names 8 different experts. In each aligned block of 128 tokens no expert is named by more than 8 tokens, a bound that some block reaches.
All inputs are finite; a program needn't handle non-finite values.
Results may differ from a plain program's by a relative error of at most 0.0051.
Values may be sent and summed in bfloat16 or wider, within the bound.
A program may use at most 128 MiB of HBM per device.

v0:
```python
import jax
import jax.numpy as jnp
from jax import lax
from jax.sharding import PartitionSpec as P

GROUP = 128


def per_device(cotangent, expert_ids, gate_values, hidden, down_weight):
    experts = lax.axis_size("expert")
    ways = lax.axis_size("dp")
    width = cotangent.shape[1]
    capacity = hidden.shape[4]
    groups_dev = hidden.shape[3]
    hidden_units = hidden.shape[5]
    window = jnp.arange(experts, dtype=jnp.int32)
    match = expert_ids[:, :, None] == window[None, None, :]
    chosen = jnp.any(match, axis=1).astype(jnp.int32).reshape(groups_dev, GROUP, experts)
    weight_sel = jnp.sum(jnp.where(match, gate_values[:, :, None], jnp.float32(0.0)), axis=1)
    weight_sel = weight_sel.reshape(groups_dev, GROUP, experts)
    rank = jnp.cumsum(chosen, axis=1) - 1
    slots = jnp.arange(capacity, dtype=jnp.int32)
    place = (rank[..., None] == slots) & (chosen[..., None] == 1)
    slot_gate = jnp.sum(jnp.where(place, weight_sel[..., None], jnp.float32(0.0)), axis=1)
    token_rows = cotangent.reshape(groups_dev, GROUP, width)
    picked = jnp.einsum(
        "jgec,jgd->ejcd", place.astype(jnp.bfloat16), token_rows, preferred_element_type=jnp.float32
    )
    routed = (picked * jnp.transpose(slot_gate, (1, 0, 2))[..., None]).astype(jnp.bfloat16)
    columns = lax.all_to_all(
        lax.all_to_all(routed[None], "expert", split_axis=1, concat_axis=1, tiled=True),
        "dp",
        split_axis=4,
        concat_axis=0,
        tiled=True,
    )
    flat_cols = columns.reshape(-1, columns.shape[4])
    grad_rows = lax.psum_scatter(
        lax.dot_general(
            flat_cols, down_weight[0], (((1,), (1,)), ((), ())), preferred_element_type=jnp.float32
        ),
        "dp",
        scatter_dimension=0,
        tiled=True,
    )
    hidden_grad = grad_rows.astype(jnp.bfloat16).reshape(hidden.shape)
    shard_width = columns.shape[4]
    empty_fisher = jnp.zeros((hidden_units, shard_width), jnp.float32)
    piece = lax.all_gather(hidden, "dp", axis=1, tiled=True)
    count = piece.shape[1]

    def turn(index, accum):
        source = index // groups_dev
        block = index % groups_dev
        block_h = lax.dynamic_index_in_dim(piece[0], source, 0, keepdims=False)
        block_h = lax.dynamic_index_in_dim(block_h, block, 1, keepdims=False).reshape(
            -1, hidden_units
        )
        block_c = lax.dynamic_index_in_dim(columns, source, 0, keepdims=False)
        block_c = lax.dynamic_index_in_dim(block_c, block, 1, keepdims=False).reshape(
            -1, shard_width
        )
        prod = lax.dot_general(
            block_h, block_c, (((0,), (0,)), ((), ())), preferred_element_type=jnp.float32
        )
        return accum + prod * prod

    fisher_sum = lax.fori_loop(0, count * groups_dev, turn, empty_fisher)
    fisher = (fisher_sum * (1.0 / (ways * groups_dev)))[None]
    return (fisher, hidden_grad)


def solution(mesh):
    in_specs = (
        P(("group", "expert", "dp"), None),
        P(("group", "expert", "dp"), None),
        P(("group", "expert", "dp"), None),
        P(("group", "expert"), "dp", None, None, None, None),
        P("expert", None, "dp"),
    )
    out_specs = (
        P(("group", "expert"), None, "dp"),
        P(("group", "expert"), "dp", None, None, None, None),
    )
    return jax.shard_map(
        per_device, mesh=mesh, in_specs=in_specs, out_specs=out_specs, check_vma=False
    )
```

profile of v0, /device:TPU:0, one launch (start us, length us, event | category | flops | bytes accessed | tf_op | source)
XLA Modules:
  0.0 210.9 jit_solution(8177170741901431970)
XLA Ops:
  7.2 0.7 fusion.10
  7.9 0.1 copy.27
  8.1 0.2 reduce_window_sum.11
  8.4 0.7 select_reduce_fusion.1
  9.2 2.6 %fusion.7 = bf16[1,4,2,8,7168]{4,3,1,2,0:T(8,128)(2,1)S(1)} fusion(bf16[2,128,7168,1]{2,1,3,0:T(8,128)(2,1)} %bitcast.49, f32[4,2,8]{2,0,1:T(4,128)S(1)} %bitcast.55, s32[2,128,4]{1,2,0:T(4,128)S(1)} %copy.28, pred[2,128,4]{1,2,0:T(4,128)(4,1)S(1)} %copy.29), kind=kOutput, calls=%fused_computation.9 | convolution fusion | flops 118374400 | bytes 4592896 | tf_op jit(solution)/shard_map/jgec,jgd->ejcd/dot_general | solution.py:26
  11.9 17.1 %all_to_all.23 = bf16[1,4,2,8,7168]{4,3,2,0,1:T(8,128)(2,1)S(1)} all-to-all(bf16[1,4,2,8,7168]{4,3,2,0,1:T(8,128)(2,1)S(1)} %copy.30), channel_id=1, replica_groups=mesh['group'=2,'expert'=4,'dp'=4] {'expert'}, dimensions={1} | all-to-all | bytes 1835008 | tf_op jit(solution)/shard_map/all_to_all | solution.py:31
  29.0 14.6 %copy.31 = bf16[1,4,2,8,7168]{3,1,2,0,4:T(4,128)(2,1)} copy(bf16[1,4,2,8,7168]{4,3,2,0,1:T(8,128)(2,1)S(1)} %all_to_all.23) | data formatting | bytes 1835008 | tf_op jit(solution)/shard_map/all_to_all | solution.py:31
  43.6 18.8 %reshape.79 = bf16[4,2,57344]{2,1,0:T(2,128)(2,1)} reshape(bf16[7168,1,2,4,8]{4,3,2,1,0:T(4,128)(2,1)} %bitcast.47) | data formatting | bytes 1835008
  62.4 4.9 %all-to-all-start.1 = ((bf16[4,2,57344]{2,1,0:T(2,128)(2,1)}), bf16[4,2,57344]{2,1,0:T(2,128)(2,1)S(1)}, u32[]{:S(2)}, u32[]{:S(2)}) async-start(bf16[4,2,57344]{2,1,0:T(2,128)(2,1)} %reshape.79), calls=%async_computation.1 | async-start | bytes 1835008 | tf_op jit(solution)/shard_map/all_to_all | solution.py:30
  67.3 32.4 %all_gather.3 = bf16[1,4,4,2,8,1024]{5,4,3,2,0,1:T(8,128)(2,1)S(1)} all-gather(bf16[1,1,4,2,8,1024]{5,4,3,2,0,1:T(8,128)(2,1)S(1)} %bitcast.53), channel_id=1, replica_groups=mesh['group'=2,'expert'=4,'dp'=4] {'dp'}, dimensions={1}, use_global_device_ids=true | all-gather | bytes 655360 | tf_op jit(solution)/shard_map/all_gather | solution.py:49
  99.7 19.4 %reshape.80 = bf16[7168,1,2,4,8]{4,3,2,1,0:T(4,128)(2,1)} reshape(bf16[4,2,57344]{2,1,0:T(2,128)(2,1)S(1)} %all-to-all-done.1) | data formatting | bytes 1835008
  119.0 17.1 %copy.32 = bf16[1,4,2,8,4,1792]{5,3,2,1,4,0:T(8,128)(2,1)S(1)} copy(bf16[1,4,2,8,4,1792]{3,1,2,5,4,0:T(4,128)(2,1)} %bitcast.48) | data formatting | bytes 1835008 | tf_op jit(solution)/shard_map/all_to_all | solution.py:30
  136.2 4.2 %fusion.8 = f32[256,1024]{1,0:T(8,128)} fusion(bf16[256,1792]{1,0:T(8,128)(2,1)S(1)} %bitcast.50, bf16[1,1024,1792]{2,1,0:T(8,128)(2,1)} %param.11), kind=kOutput, calls=%fused_computation.11 | convolution fusion | flops 939524096 | bytes 5636096 | tf_op jit(solution)/shard_map/dot_general | solution.py:39
  140.4 55.5 %while.17 = (s32[]{:T(128)}, f32[1024,1792]{1,0:T(8,128)}, bf16[1,4,4,2,8,1024]{5,4,3,2,1,0:T(8,128)(2,1)S(1)}, bf16[4,4,2,8,1792]{4,3,2,1,0:T(8,128)(2,1)S(1)},...) while((s32[]{:T(128)}, f32[1024,1792]{1,0:T(8,128)}, ...), condition=%wide.region_5.6_spmd.clone, body=%wide.region_4.5_spmd.clone.sunk | while | flops 122945560 | bytes 14863173 | solution.py:68
  140.4 4.2 %select_add_fusion.2 = f32[1024,1792]{1,0:T(8,128)} fusion(f32[1024,1792]{1,0:T(8,128)} %get-tuple-element.208, pred[]{:T(512)S(6)} %compare.16, bf16[4,4,2,8,1792]{4,3,2,1,0:T(8,128)(2,1)S(1)} %get-tuple-element.220, s32[]{:T(128)S(6)} %select_n.92, s32[]{:T(128)S(6)} %select_n.95, bf16[1,4,4,2,8,1024]{5,4,3,2,1,0:T(8,128)(2,1)S(1)} %get-tuple-element.219), kind=kOutput, calls=%fused_computation.clone.1 | convolution fusion | flops 122945536 | bytes 14862848 | tf_op jit(solution)/shard_map/while/body/eval_jaxpr/dot_general | solution.py:63
  144.6 7.4 %select_add_fusion.2 = f32[1024,1792]{1,0:T(8,128)} fusion(f32[1024,1792]{1,0:T(8,128)} %get-tuple-element.208, pred[]{:T(512)S(6)} %compare.16, bf16[4,4,2,8,1792]{4,3,2,1,0:T(8,128)(2,1)S(1)} %get-tuple-element.220, s32[]{:T(128)S(6)} %select_n.92, s32[]{:T(128)S(6)} %select_n.95, bf16[1,4,4,2,8,1024]{5,4,3,2,1,0:T(8,128)(2,1)S(1)} %get-tuple-element.219), kind=kOutput, calls=%fused_computation.clone.1 | convolution fusion | flops 122945536 | bytes 14862848 | tf_op jit(solution)/shard_map/while/body/eval_jaxpr/dot_general | solution.py:63
  152.1 7.3 %select_add_fusion.2 = f32[1024,1792]{1,0:T(8,128)} fusion(f32[1024,1792]{1,0:T(8,128)} %get-tuple-element.208, pred[]{:T(512)S(6)} %compare.16, bf16[4,4,2,8,1792]{4,3,2,1,0:T(8,128)(2,1)S(1)} %get-tuple-element.220, s32[]{:T(128)S(6)} %select_n.92, s32[]{:T(128)S(6)} %select_n.95, bf16[1,4,4,2,8,1024]{5,4,3,2,1,0:T(8,128)(2,1)S(1)} %get-tuple-element.219), kind=kOutput, calls=%fused_computation.clone.1 | convolution fusion | flops 122945536 | bytes 14862848 | tf_op jit(solution)/shard_map/while/body/eval_jaxpr/dot_general | solution.py:63
  159.4 7.3 %select_add_fusion.2 = f32[1024,1792]{1,0:T(8,128)} fusion(f32[1024,1792]{1,0:T(8,128)} %get-tuple-element.208, pred[]{:T(512)S(6)} %compare.16, bf16[4,4,2,8,1792]{4,3,2,1,0:T(8,128)(2,1)S(1)} %get-tuple-element.220, s32[]{:T(128)S(6)} %select_n.92, s32[]{:T(128)S(6)} %select_n.95, bf16[1,4,4,2,8,1024]{5,4,3,2,1,0:T(8,128)(2,1)S(1)} %get-tuple-element.219), kind=kOutput, calls=%fused_computation.clone.1 | convolution fusion | flops 122945536 | bytes 14862848 | tf_op jit(solution)/shard_map/while/body/eval_jaxpr/dot_general | solution.py:63
  166.7 7.3 %select_add_fusion.2 = f32[1024,1792]{1,0:T(8,128)} fusion(f32[1024,1792]{1,0:T(8,128)} %get-tuple-element.208, pred[]{:T(512)S(6)} %compare.16, bf16[4,4,2,8,1792]{4,3,2,1,0:T(8,128)(2,1)S(1)} %get-tuple-element.220, s32[]{:T(128)S(6)} %select_n.92, s32[]{:T(128)S(6)} %select_n.95, bf16[1,4,4,2,8,1024]{5,4,3,2,1,0:T(8,128)(2,1)S(1)} %get-tuple-element.219), kind=kOutput, calls=%fused_computation.clone.1 | convolution fusion | flops 122945536 | bytes 14862848 | tf_op jit(solution)/shard_map/while/body/eval_jaxpr/dot_general | solution.py:63
  174.0 7.3 %select_add_fusion.2 = f32[1024,1792]{1,0:T(8,128)} fusion(f32[1024,1792]{1,0:T(8,128)} %get-tuple-element.208, pred[]{:T(512)S(6)} %compare.16, bf16[4,4,2,8,1792]{4,3,2,1,0:T(8,128)(2,1)S(1)} %get-tuple-element.220, s32[]{:T(128)S(6)} %select_n.92, s32[]{:T(128)S(6)} %select_n.95, bf16[1,4,4,2,8,1024]{5,4,3,2,1,0:T(8,128)(2,1)S(1)} %get-tuple-element.219), kind=kOutput, calls=%fused_computation.clone.1 | convolution fusion | flops 122945536 | bytes 14862848 | tf_op jit(solution)/shard_map/while/body/eval_jaxpr/dot_general | solution.py:63
  181.3 7.3 %select_add_fusion.2 = f32[1024,1792]{1,0:T(8,128)} fusion(f32[1024,1792]{1,0:T(8,128)} %get-tuple-element.208, pred[]{:T(512)S(6)} %compare.16, bf16[4,4,2,8,1792]{4,3,2,1,0:T(8,128)(2,1)S(1)} %get-tuple-element.220, s32[]{:T(128)S(6)} %select_n.92, s32[]{:T(128)S(6)} %select_n.95, bf16[1,4,4,2,8,1024]{5,4,3,2,1,0:T(8,128)(2,1)S(1)} %get-tuple-element.219), kind=kOutput, calls=%fused_computation.clone.1 | convolution fusion | flops 122945536 | bytes 14862848 | tf_op jit(solution)/shard_map/while/body/eval_jaxpr/dot_general | solution.py:63
  188.6 7.3 %select_add_fusion.2 = f32[1024,1792]{1,0:T(8,128)} fusion(f32[1024,1792]{1,0:T(8,128)} %get-tuple-element.208, pred[]{:T(512)S(6)} %compare.16, bf16[4,4,2,8,1792]{4,3,2,1,0:T(8,128)(2,1)S(1)} %get-tuple-element.220, s32[]{:T(128)S(6)} %select_n.92, s32[]{:T(128)S(6)} %select_n.95, bf16[1,4,4,2,8,1024]{5,4,3,2,1,0:T(8,128)(2,1)S(1)} %get-tuple-element.219), kind=kOutput, calls=%fused_computation.clone.1 | convolution fusion | flops 122945536 | bytes 14862848 | tf_op jit(solution)/shard_map/while/body/eval_jaxpr/dot_general | solution.py:63
  195.9 6.6 %multiply_bitcast_fusion = f32[1,1024,1792]{2,1,0:T(8,128)} fusion(f32[1024,1792]{1,0:T(8,128)} %get-tuple-element.140), kind=kLoop, calls=%fused_computation.10 | loop fusion | flops 1835008 | bytes 14680064 | tf_op jit(solution)/shard_map/broadcast_in_dim | solution.py:69
  202.5 1.6 convert_element_type.26
  (15 shorter events, 0.3 us)
Async XLA Ops:
  43.6 23.7 %copy-start = (bf16[1,1,4,2,8,1024]{5,4,3,2,1,0:T(8,128)(2,1)S(1)}, bf16[1,1,4,2,8,1024]{5,4,3,2,1,0:T(8,128)(2,1)}, u32[]{:S(2)}) copy-start(bf16[1,1,4,2,8,1024]{5,4,3,2,1,0:T(8,128)(2,1)} %param.10) | copy-start | bytes 393220
  62.4 37.3 %all-to-all-start.1 = ((bf16[4,2,57344]{2,1,0:T(2,128)(2,1)}), bf16[4,2,57344]{2,1,0:T(2,128)(2,1)S(1)}, u32[]{:S(2)}, u32[]{:S(2)}) async-start(bf16[4,2,57344]{2,1,0:T(2,128)(2,1)} %reshape.79), calls=%async_computation.1 | async-start | bytes 1835008 | tf_op jit(solution)/shard_map/all_to_all | solution.py:30
  67.2 135.2 %reduce-scatter.2.cloned.1.call-start = ((), (), s32[]{:S(2)}) async-start(), calls=%async_computation.3 | async-start | bytes 1310720 | tf_op jit(solution)/shard_map/reduce_scatter | solution.py:38
Sparse Core Ops, SparseCore 0:
  140.5 27.8 reduce-scatter.1
where the time goes:
time: 212 us; the launch traced here: 211 us
  local copies, waits for them, and re-layouts  70.2 us (33%)
  matrix products  62.3 us (29%)
  blocking collectives  49.5 us (23%)
  between operations  14.1 us (7%)
  other arithmetic  10 us (5%)
  starting transfers between devices  4.87 us (2%)
    dot_general x8, matrix products, turn(): lax.dot_general(block_h, block_c, (((0,), (0,)), ((), ())), preferred_ele...  55.4 us
    unnamed x4, local copies, waits for them, and re-layouts  38.2 us
    all_gather x1, blocking collectives, per_device(): piece = lax.all_gather(hidden, 'dp', axis=1, tiled=True)  32.4 us
    all_to_all x1, local copies, waits for them, and re-layouts, per_device(): lax.all_to_all(lax.all_to_all(routed[None], 'expert', split_axis=1, conca...  17.1 us
    all_to_all x1, blocking collectives, per_device(): lax.all_to_all(routed[None], 'expert', split_axis=1, concat_axis=1, tiled...  17.1 us
    all_to_all x1, local copies, waits for them, and re-layouts, per_device(): lax.all_to_all(routed[None], 'expert', split_axis=1, concat_axis=1, tiled...  14.6 us
    broadcast_in_dim x1, other arithmetic, per_device(): fisher = (fisher_sum * (1.0 / (ways * groups_dev)))[None]  6.6 us
    all_to_all x1, starting transfers between devices, per_device(): lax.all_to_all(lax.all_to_all(routed[None], 'expert', split_axis=1, conca...  4.87 us
  transfers between devices with their start and end apart: 2, of which 0 were waited for; matrix products, arithmetic and copies ran while one was open for 29% of the time, Pallas kernels for 0%

commit v1 on v0

v1 whole, which is shorter than its diff:
```python
import functools

import jax
import jax.numpy as jnp
from jax import lax
from jax.experimental import pallas as pl
from jax.experimental.pallas import tpu as pltpu
from jax.sharding import PartitionSpec as P

GROUP = 128
MESH = pl.DeviceIdType.MESH


def partner(index, step, size):
    out, bit = 0, 1
    while bit < size:
        digit = (index // bit) % 2
        out = out + bit * ((1 - digit) if step & bit else digit)
        bit *= 2
    return out


def place_rows(ids, gates, experts, groups, cap):
    tokens, top = ids.shape
    slots = experts * groups * cap
    lanes = max(slots, 128)
    lane = lax.broadcasted_iota(jnp.int32, (tokens, lanes), 1)
    token = lax.broadcasted_iota(jnp.int32, (tokens, lanes), 0)
    lane_e = lax.div(lane, groups * cap)
    lane_j = lax.rem(lax.div(lane, cap), groups)
    lane_c = lax.rem(lane, cap).astype(jnp.float32)
    chosen = jnp.zeros((tokens, lanes), jnp.float32)
    gate = jnp.zeros((tokens, lanes), jnp.float32)
    for k in range(top):
        same = ids[:, k : k + 1] == lane_e
        chosen = chosen + jnp.where(same, 1.0, 0.0)
        gate = gate + jnp.where(same, gates[:, k : k + 1], 0.0)
    row = lax.broadcasted_iota(jnp.int32, (tokens, tokens), 0)
    col = lax.broadcasted_iota(jnp.int32, (tokens, tokens), 1)
    before = (col < row) & (lax.div(col, GROUP) == lax.div(row, GROUP))
    rank = jnp.dot(
        jnp.where(before, 1.0, 0.0).astype(jnp.bfloat16),
        chosen.astype(jnp.bfloat16),
        preferred_element_type=jnp.float32,
    )
    taken = (chosen > 0.5) & (rank == lane_c) & (lax.div(token, GROUP) == lane_j)
    place = jnp.where(taken, 1.0, 0.0)
    turned = place.T[:slots]
    slot_gate = jnp.sum(jnp.where(taken, gate, 0.0).T, axis=1, keepdims=True)[:slots]
    return turned.astype(jnp.bfloat16), slot_gate


def route_kernel(
    experts, ways, groups, cap,
    ids_ref, gates_ref, cot_hbm, hid_hbm, w_hbm,
    cols_hbm, hid_out, grad_ref,
    cot, w, routed, cols, hidden, part_out, part_in, own,
    cot_sem, w_sem, hid_sem, own_sem, out_sem,
    send_sem, recv_sem, hsend_sem, hrecv_sem, psend_sem, precv_sem,
):
    g, f, d = lax.axis_index("group"), lax.axis_index("expert"), lax.axis_index("dp")
    piece = groups * cap
    units = w.shape[0]
    width = w.shape[1]
    order = list(range(ways - 1, -1, -1))
    peers = [partner(d, k, ways) for k in range(ways)]

    def cot_copy(k):
        columns = pl.ds(pl.multiple_of(peers[k] * width, width), width)
        return pltpu.make_async_copy(cot_hbm.at[:, columns], cot.at[k], cot_sem.at[k])

    hid_copy = pltpu.make_async_copy(hid_hbm, hidden.at[d], hid_sem)
    w_copy = pltpu.make_async_copy(w_hbm, w, w_sem)
    hid_copy.start()
    for k in order:
        cot_copy(k).start()
    w_copy.start()

    barrier = pltpu.get_barrier_semaphore()
    total = experts * ways

    def greet(i, carry):
        other = (f * ways + d + i) % total
        pl.semaphore_signal(
            barrier, inc=1, device_id=(g, other // ways, other % ways), device_id_type=MESH
        )
        return carry

    lax.fori_loop(1, total, greet, 0)
    place, slot_gate = place_rows(ids_ref[...], gates_ref[...], experts, groups, cap)
    pl.semaphore_wait(barrier, total - 1)

    def hid_send(k):
        return pltpu.make_async_remote_copy(
            src_ref=hidden.at[d], dst_ref=hidden.at[d],
            send_sem=hsend_sem.at[k], recv_sem=hrecv_sem.at[k],
            device_id=(g, f, peers[k]), device_id_type=MESH,
        )

    def row_send(k, i):
        e = (f + i) % experts
        rows = pl.ds(pl.multiple_of(e * piece, piece), piece)
        mine = pl.ds(pl.multiple_of(f * piece, piece), piece)
        return pltpu.make_async_remote_copy(
            src_ref=routed.at[k, rows], dst_ref=cols.at[d, mine],
            send_sem=send_sem.at[k, i], recv_sem=recv_sem.at[k, i],
            device_id=(g, e, peers[k]), device_id_type=MESH,
        )

    def row_wait(k, i):
        source = (f + experts - i) % experts
        rows = pl.ds(pl.multiple_of(source * piece, piece), piece)
        return pltpu.make_async_remote_copy(
            src_ref=routed.at[k, rows], dst_ref=cols.at[peers[k], rows],
            send_sem=send_sem.at[k, i], recv_sem=recv_sem.at[k, i],
            device_id=(g, source, peers[k]), device_id_type=MESH,
        )

    hid_copy.wait()
    for k in order:
        if k:
            hid_send(k).start()

    chunk = 256 if width % 256 == 0 else 128
    mine = pl.ds(pl.multiple_of(f * piece, piece), piece)
    own_copy = pltpu.make_async_copy(routed.at[0, mine], cols.at[d, mine], own_sem)
    for k in order:
        cot_copy(k).wait()

        @pl.loop(0, width // chunk)
        def pick(n):
            at = pl.ds(pl.multiple_of(n * chunk, chunk), chunk)
            picked = jnp.dot(place, cot[k, :, at], preferred_element_type=jnp.float32)
            routed[k, :, at] = (picked * slot_gate).astype(jnp.bfloat16)

        for i in range(experts):
            if k or i:
                row_send(k, i).start()
            else:
                own_copy.start()

    w_copy.wait()
    tile = 256

    def part_send(k):
        return pltpu.make_async_remote_copy(
            src_ref=part_out.at[k], dst_ref=part_in.at[k],
            send_sem=psend_sem.at[k], recv_sem=precv_sem.at[k],
            device_id=(g, f, peers[k]), device_id_type=MESH,
        )

    def cols_out(k):
        return pltpu.make_async_copy(cols.at[peers[k]], cols_hbm.at[peers[k]], out_sem.at[0, k])

    def hid_back(k):
        return pltpu.make_async_copy(hidden.at[peers[k]], hid_out.at[peers[k]], out_sem.at[1, k])

    def hid_wait(k):
        return pltpu.make_async_remote_copy(
            src_ref=hidden.at[peers[k]], dst_ref=hidden.at[peers[k]],
            send_sem=hsend_sem.at[k], recv_sem=hrecv_sem.at[k],
            device_id=(g, f, peers[k]), device_id_type=MESH,
        )

    for k in order:
        for i in range(experts):
            if k or i:
                row_wait(k, i).wait_recv()
            else:
                own_copy.wait()
        cols_out(k).start()

        @pl.loop(0, units // tile)
        def multiply(n):
            at = pl.ds(pl.multiple_of(n * tile, tile), tile)
            part = lax.dot_general(
                cols[peers[k]], w[at, :], (((1,), (1,)), ((), ())),
                preferred_element_type=jnp.float32,
            )
            if k:
                part_out[k, :, at] = part.astype(jnp.bfloat16)
            else:
                own[:, at] = part

        if k:
            part_send(k).start()

    for k in order:
        if k:
            hid_wait(k).wait_recv()
        hid_back(k).start()
    acc = own[...]
    for k in order:
        if k:
            part_send(k).wait_recv()
            acc = acc + part_in[k].astype(jnp.float32)
    grad_ref[...] = acc.astype(jnp.bfloat16)
    for k in order:
        cols_out(k).wait()
        hid_back(k).wait()
        for i in range(experts):
            if k or i:
                row_send(k, i).wait_send()
        if k:
            hid_send(k).wait_send()
            part_send(k).wait_send()


def fisher_kernel(groups, cap, scale, cols_ref, hid_ref, out_ref):
    ways, rows, width = cols_ref.shape
    tile = out_ref.shape[0]
    lane = lax.broadcasted_iota(jnp.int32, (tile, rows), 1)
    lane_j = lax.rem(lax.div(lane, cap), groups)
    turned = [hid_ref[s].astype(jnp.float32).T for s in range(ways)]
    lhs = [
        [jnp.where(lane_j == j, turned[s], 0.0).astype(jnp.bfloat16) for j in range(groups)]
        for s in range(ways)
    ]
    chunk = 256 if width % 256 == 0 else 128
    for n in range(width // chunk):
        at = slice(n * chunk, (n + 1) * chunk)
        acc = jnp.zeros((tile, chunk), jnp.float32)
        for s in range(ways):
            for j in range(groups):
                prod = jnp.dot(lhs[s][j], cols_ref[s, :, at], preferred_element_type=jnp.float32)
                acc = acc + prod * prod
        out_ref[:, at] = acc * scale


def per_device(cotangent, expert_ids, gate_values, hidden, down_weight):
    experts = lax.axis_size("expert")
    ways = lax.axis_size("dp")
    groups, cap, units = hidden.shape[3], hidden.shape[4], hidden.shape[5]
    piece = groups * cap
    slots = experts * piece
    width = down_weight.shape[2]
    tokens = cotangent.shape[0]
    any_spec = pl.BlockSpec(memory_space=pl.ANY)
    vmem_spec = pl.BlockSpec(memory_space=pltpu.VMEM)
    bf16 = jnp.bfloat16
    columns, gathered, grad = pl.pallas_call(
        functools.partial(route_kernel, experts, ways, groups, cap),
        out_shape=(
            jax.ShapeDtypeStruct((ways, slots, width), bf16),
            jax.ShapeDtypeStruct((ways, slots, units), bf16),
            jax.ShapeDtypeStruct((slots, units), bf16),
        ),
        in_specs=[vmem_spec, vmem_spec, any_spec, any_spec, any_spec],
        out_specs=(any_spec, any_spec, vmem_spec),
        scratch_shapes=[
            pltpu.VMEM((ways, tokens, width), bf16),
            pltpu.VMEM((units, width), bf16),
            pltpu.VMEM((ways, slots, width), bf16),
            pltpu.VMEM((ways, slots, width), bf16),
            pltpu.VMEM((ways, slots, units), bf16),
            pltpu.VMEM((ways, slots, units), bf16),
            pltpu.VMEM((ways, slots, units), bf16),
            pltpu.VMEM((slots, units), jnp.float32),
            pltpu.SemaphoreType.DMA((ways,)),
            pltpu.SemaphoreType.DMA,
            pltpu.SemaphoreType.DMA,
            pltpu.SemaphoreType.DMA,
            pltpu.SemaphoreType.DMA((2, ways)),
            pltpu.SemaphoreType.DMA((ways, experts)),
            pltpu.SemaphoreType.DMA((ways, experts)),
            pltpu.SemaphoreType.DMA((ways,)),
            pltpu.SemaphoreType.DMA((ways,)),
            pltpu.SemaphoreType.DMA((ways,)),
            pltpu.SemaphoreType.DMA((ways,)),
        ],
        compiler_params=pltpu.CompilerParams(
            collective_id=0, has_side_effects=True, vmem_limit_bytes=48 * 2**20
        ),
        name="route",
    )(expert_ids, gate_values, cotangent, hidden.reshape(slots, units), down_weight[0])
    tile = 128
    fisher = pl.pallas_call(
        functools.partial(fisher_kernel, groups, cap, 1.0 / (ways * groups)),
        out_shape=jax.ShapeDtypeStruct((units, width), jnp.float32),
        grid=(units // tile,),
        in_specs=[
            pl.BlockSpec((ways, slots, width), lambda i: (0, 0, 0)),
            pl.BlockSpec((ways, slots, tile), lambda i: (0, 0, i)),
        ],
        out_specs=pl.BlockSpec((tile, width), lambda i: (i, 0)),
        compiler_params=pltpu.CompilerParams(vmem_limit_bytes=32 * 2**20),
        name="fisher",
    )(columns, gathered)
    return (fisher[None], grad.reshape(hidden.shape))


def solution(mesh):
    in_specs = (
        P(("group", "expert", "dp"), None),
        P(("group", "expert", "dp"), None),
        P(("group", "expert", "dp"), None),
        P(("group", "expert"), "dp", None, None, None, None),
        P("expert", None, "dp"),
    )
    out_specs = (
        P(("group", "expert"), None, "dp"),
        P(("group", "expert"), "dp", None, None, None, None),
    )
    return jax.shard_map(
        per_device, mesh=mesh, in_specs=in_specs, out_specs=out_specs, check_vma=False
    )
```

time: 212 us -> 67.8 us (0.32)
  local copies, waits for them, and re-layouts: 70.2 us -> 5.24 us
  matrix products: 62.3 us -> 0 us
  Pallas kernels: 0 us -> 61.6 us
  blocking collectives: 49.5 us -> 0 us
  between operations: 14.1 us -> 0.66 us
  other arithmetic: 10 us -> 0 us
  starting transfers between devices: 4.87 us -> 0 us
    dot_general x10 -> x0, matrix products: 62.3 us -> none  [the longest x8 55.4 us: turn(): lax.dot_general(block_h, block_c, (((0,), (0,)), ((), ())), preferred_ele...]
    pallas_call x0 -> x2, Pallas kernels: none -> 61.6 us  [the longest x1 51 us: per_device(): pl.pallas_call(functools.partial(route_kernel, experts, ways, groups, cap...]
    unnamed x4 -> x7, local copies, waits for them, and re-layouts: 38.2 us -> 5.24 us
    all_gather x1 -> x0, blocking collectives: 32.4 us -> none  [per_device(): piece = lax.all_gather(hidden, 'dp', axis=1, tiled=True)]
    all_to_all x2 -> x0, local copies, waits for them, and re-layouts: 31.8 us -> none  [the longest x1 17.1 us: per_device(): lax.all_to_all(lax.all_to_all(routed[None], 'expert', split_axis=1, conca...]
    all_to_all x1 -> x0, blocking collectives: 17.1 us -> none  [per_device(): lax.all_to_all(routed[None], 'expert', split_axis=1, concat_axis=1, tiled...]
    broadcast_in_dim x1 -> x0, other arithmetic: 6.6 us -> none  [per_device(): fisher = (fisher_sum * (1.0 / (ways * groups_dev)))[None]]
    all_to_all x1 -> x0, starting transfers between devices: 4.87 us -> none  [per_device(): lax.all_to_all(lax.all_to_all(routed[None], 'expert', split_axis=1, conca...]
  transfers between devices with their start and end apart: 2 -> 0, of which waited for: 0 -> 0; matrix products, arithmetic and copies ran while one was open for 29% -> 0% of each run, Pallas kernels for 0% -> 0%
where the time goes in v1:
time: 67.8 us; the launch traced here: 67.5 us
  Pallas kernels  61.6 us (91%)
  local copies, waits for them, and re-layouts  5.24 us (8%)
    pallas_call x1, Pallas kernels, per_device(): pl.pallas_call(functools.partial(route_kernel, experts, ways, groups, cap...  51 us
    pallas_call x1, Pallas kernels, per_device(): pl.pallas_call(functools.partial(fisher_kernel, groups, cap, 1.0 / (ways...  10.5 us
    unnamed x7, local copies, waits for them, and re-layouts  5.24 us

profile of v1, /device:TPU:0, one launch (start us, length us, event | category | flops | bytes accessed | tf_op | source)
XLA Modules:
  0.0 67.5 jit_solution(1272228685133342864)
XLA Ops:
  0.6 0.8 %copy.7.ids_ref = s32[256,8]{1,0:T(8,128)S(1)} copy(s32[256,8]{0,1:T(8,128)} %param.6) | data formatting | bytes 16384 | tf_op args[1]
  1.5 0.8 %copy.8.gates_ref = f32[256,8]{1,0:T(8,128)S(1)} copy(f32[256,8]{0,1:T(8,128)} %param.7) | data formatting | bytes 16384 | tf_op args[2]
  2.3 0.0 copy-start
  2.3 2.0 %copy-done = bf16[256,7168]{1,0:T(8,128)(2,1)S(1)} copy-done((bf16[256,7168]{1,0:T(8,128)(2,1)S(1)}, bf16[256,7168]{1,0:T(8,128)(2,1)}, u32[]{:S(2)}) %copy-start) | copy-done | bytes 3670040
  4.3 0.0 copy-start.1
  4.3 0.9 %copy-done.1 = bf16[1,1,4,2,8,1024]{5,4,3,2,1,0:T(8,128)(2,1)S(1)} copy-done((bf16[1,1,4,2,8,1024]{5,4,3,2,1,0:T(8,128)(2,1)S(1)}, bf16[1,1,4,2,8,1024]{5,4,3,2,1,0:T(8,128)(2,1)}, u32[]{:S(2)}) %copy-start.1) | copy-done | bytes 131096
  5.2 51.0 %route.1 = (bf16[4,64,1792]{2,1,0:T(8,128)(2,1)S(1)}, bf16[4,64,1024]{2,1,0:T(8,128)(2,1)S(1)}, bf16[64,1024]{1,0:T(8,128)(2,1)S(1)}) custom-call(s32[256,8]{1,0:T(8,128)S(1)} %copy.7.ids_ref, f32[256,8]{1,0:T(8,128)S(1)} %copy.8.gates_ref, bf16[256,7168]{1,0:T(8,128)(2,1)S(1)} %copy-done, bf16[64,1024]{1,0:T(8,128)(2,1)S(1)} %bitcast.4, ...), custom_call_target="tpu_custom_call" | custom-call | tf_op jit(solution)/shard_map/route/pallas_call | solution.py:241
  56.3 10.5 %fisher.1 = f32[1024,1792]{1,0:T(8,128)} custom-call(bf16[4,64,1792]{2,1,0:T(8,128)(2,1)S(1)} %get-tuple-element.5.cols_ref, bf16[4,64,1024]{2,1,0:T(8,128)(2,1)S(1)} %get-tuple-element.6.hid_ref), custom_call_target="tpu_custom_call" | custom-call | tf_op jit(solution)/shard_map/fisher/pallas_call | solution.py:277
  66.8 0.7 copy.10
Async XLA Ops:
  2.3 2.0 %copy-start = (bf16[256,7168]{1,0:T(8,128)(2,1)S(1)}, bf16[256,7168]{1,0:T(8,128)(2,1)}, u32[]{:S(2)}) copy-start(bf16[256,7168]{1,0:T(8,128)(2,1)} %cot_hbm.1) | copy-start | bytes 11010052
  4.3 0.9 %copy-start.1 = (bf16[1,1,4,2,8,1024]{5,4,3,2,1,0:T(8,128)(2,1)S(1)}, bf16[1,1,4,2,8,1024]{5,4,3,2,1,0:T(8,128)(2,1)}, u32[]{:S(2)}) copy-start(bf16[1,1,4,2,8,1024]{5,4,3,2,1,0:T(8,128)(2,1)} %param.8) | copy-start | bytes 393220

commit v2 on v1

v2 whole, which is shorter than its diff:
```python
import functools

import jax
import jax.numpy as jnp
from jax import lax
from jax.experimental import pallas as pl
from jax.experimental.pallas import tpu as pltpu
from jax.sharding import PartitionSpec as P

GROUP = 128
MESH = pl.DeviceIdType.MESH


def partner(index, step, size):
    out, bit = 0, 1
    while bit < size:
        digit = (index // bit) % 2
        out = out + bit * ((1 - digit) if step & bit else digit)
        bit *= 2
    return out


def place_rows(ids, gates, experts, groups, cap):
    top, tokens = ids.shape
    slots = experts * groups * cap
    slot = lax.broadcasted_iota(jnp.int32, (slots, tokens), 0)
    token = lax.broadcasted_iota(jnp.int32, (slots, tokens), 1)
    slot_e = lax.div(slot, groups * cap)
    slot_j = lax.rem(lax.div(slot, cap), groups)
    slot_c = lax.rem(slot, cap).astype(jnp.float32)
    chosen = jnp.zeros((slots, tokens), jnp.float32)
    gate = jnp.zeros((slots, tokens), jnp.float32)
    for k in range(top):
        same = ids[k : k + 1, :] == slot_e
        chosen = chosen + jnp.where(same, 1.0, 0.0)
        gate = gate + jnp.where(same, gates[k : k + 1, :], 0.0)
    row = lax.broadcasted_iota(jnp.int32, (tokens, tokens), 0)
    col = lax.broadcasted_iota(jnp.int32, (tokens, tokens), 1)
    before = (row < col) & (lax.div(col, GROUP) == lax.div(row, GROUP))
    rank = jnp.dot(
        chosen.astype(jnp.bfloat16),
        jnp.where(before, 1.0, 0.0).astype(jnp.bfloat16),
        preferred_element_type=jnp.float32,
    )
    taken = (chosen > 0.5) & (rank == slot_c) & (lax.div(token, GROUP) == slot_j)
    slot_gate = jnp.sum(jnp.where(taken, gate, 0.0), axis=1, keepdims=True)
    return jnp.where(taken, 1.0, 0.0).astype(jnp.bfloat16), slot_gate


def lowest(k):
    return k & -k


def route_kernel(
    experts, ways, groups, cap,
    ids_hbm, gates_hbm, cot_hbm, hid_hbm, w_hbm,
    fisher_ref, grad_ref,
    ids, gates, cot, w, routed, cols, hidden, part_out, part_in, acc, turned,
    small_sem, cot_sem, w_sem, hid_sem, own_sem,
    send_sem, recv_sem, hsend_sem, hrecv_sem, psend_sem, precv_sem,
):
    g, f, d = lax.axis_index("group"), lax.axis_index("expert"), lax.axis_index("dp")
    piece = groups * cap
    units, width = w.shape
    slots = experts * piece
    order = list(range(ways - 1, -1, -1))
    peers = [partner(d, k, ways) for k in range(ways)]

    def cot_copy(k):
        columns = pl.ds(pl.multiple_of(peers[k] * width, width), width)
        return pltpu.make_async_copy(cot_hbm.at[:, columns], cot.at[k], cot_sem.at[k])

    ids_copy = pltpu.make_async_copy(ids_hbm, ids, small_sem.at[0])
    gates_copy = pltpu.make_async_copy(gates_hbm, gates, small_sem.at[1])
    hid_copy = pltpu.make_async_copy(hid_hbm, hidden.at[0], hid_sem)
    w_copy = pltpu.make_async_copy(w_hbm, w, w_sem)
    ids_copy.start()
    gates_copy.start()
    hid_copy.start()
    for k in order:
        cot_copy(k).start()
    w_copy.start()

    barrier = pltpu.get_barrier_semaphore()
    total = experts * ways

    def greet(i, carry):
        other = (f * ways + d + i) % total
        pl.semaphore_signal(
            barrier, inc=1, device_id=(g, other // ways, other % ways), device_id_type=MESH
        )
        return carry

    lax.fori_loop(1, total, greet, 0)
    ids_copy.wait()
    gates_copy.wait()
    place, slot_gate = place_rows(ids[...], gates[...], experts, groups, cap)
    hid_copy.wait()
    pl.semaphore_wait(barrier, total - 1)

    def hid_send(k):
        return pltpu.make_async_remote_copy(
            src_ref=hidden.at[k - lowest(k)], dst_ref=hidden.at[k],
            send_sem=hsend_sem.at[k], recv_sem=hrecv_sem.at[k],
            device_id=(g, f, peers[lowest(k)]), device_id_type=MESH,
        )

    def part_send(k):
        return pltpu.make_async_remote_copy(
            src_ref=part_out.at[k], dst_ref=part_in.at[k],
            send_sem=psend_sem.at[k], recv_sem=precv_sem.at[k],
            device_id=(g, f, peers[lowest(k)]), device_id_type=MESH,
        )

    def row_send(k, i):
        e = (f + i) % experts
        rows = pl.ds(pl.multiple_of(e * piece, piece), piece)
        mine = pl.ds(pl.multiple_of(f * piece, piece), piece)
        return pltpu.make_async_remote_copy(
            src_ref=routed.at[k, rows], dst_ref=cols.at[k, mine],
            send_sem=send_sem.at[k, i], recv_sem=recv_sem.at[k, i],
            device_id=(g, e, peers[k]), device_id_type=MESH,
        )

    def row_wait(k, i):
        source = (f + experts - i) % experts
        rows = pl.ds(pl.multiple_of(source * piece, piece), piece)
        return pltpu.make_async_remote_copy(
            src_ref=routed.at[k, rows], dst_ref=cols.at[k, rows],
            send_sem=send_sem.at[k, i], recv_sem=recv_sem.at[k, i],
            device_id=(g, source, peers[k]), device_id_type=MESH,
        )

    gather = sorted(range(1, ways), key=lambda k: -lowest(k))
    for k in gather:
        if k == lowest(k):
            hid_send(k).start()

    chunk = 256 if width % 256 == 0 else 128
    mine = pl.ds(pl.multiple_of(f * piece, piece), piece)
    own_copy = pltpu.make_async_copy(routed.at[0, mine], cols.at[0, mine], own_sem)
    for k in order:
        cot_copy(k).wait()
        for n in range(width // chunk):
            at = slice(n * chunk, (n + 1) * chunk)
            picked = jnp.dot(place, cot[k, :, at], preferred_element_type=jnp.float32)
            routed[k, :, at] = (picked * slot_gate).astype(jnp.bfloat16)
        for i in range(experts):
            if k or i:
                row_send(k, i).start()
            else:
                own_copy.start()

    arrived = set()

    def hid_arrive(k):
        if k and k not in arrived:
            hid_send(k).wait_recv()
            arrived.add(k)

    for k in gather:
        if k != lowest(k):
            hid_arrive(k - lowest(k))
            hid_send(k).start()

    w_copy.wait()
    tile = 256
    lane = lax.broadcasted_iota(jnp.int32, (units, 2 * slots), 1)
    lane_j = lax.rem(lax.div(lane, cap), groups)
    lane_half = lax.div(lane, slots)
    scale = 1.0 / (ways * groups)

    def combine(k):
        part_send(k).wait_recv()
        acc[k - lowest(k)] += part_in[k].astype(jnp.float32)

    def send_part(k):
        part_out[k] = acc[k].astype(jnp.bfloat16)
        part_send(k).start()

    for first in range(0, ways, 2):
        for k in (first + 1, first):
            for i in range(experts):
                if k or i:
                    row_wait(k, i).wait_recv()
                else:
                    own_copy.wait()

        pair = cols[first : first + 2].reshape(2 * slots, width)
        for n in range(units // tile):
            at = slice(n * tile, (n + 1) * tile)
            part = lax.dot_general(
                pair, w[at, :], (((1,), (1,)), ((), ())), preferred_element_type=jnp.float32
            )
            acc[first, :, at] = part[:slots]
            part_out[first + 1, :, at] = part[slots:].astype(jnp.bfloat16)
        part_send(first + 1).start()

        if first + 2 == ways:
            for k in range(ways - 2, 0, -2):
                combine(k + 1)
                if lowest(k) == 2:
                    send_part(k)

        hid_arrive(first + 1)
        hid_arrive(first)
        flat = hidden[first : first + 2].reshape(2 * slots, units).astype(jnp.float32).T
        for h in range(2):
            for j in range(groups):
                keep = (lane_half == h) & (lane_j == j)
                turned[h * groups + j] = jnp.where(keep, flat, 0.0).astype(jnp.bfloat16)

        @pl.loop(0, width // chunk)
        def squares(n):
            at = pl.ds(pl.multiple_of(n * chunk, chunk), chunk)
            block = cols[first : first + 2, :, at].reshape(2 * slots, chunk)
            step = 128
            for m in range(units // step):
                rows = slice(m * step, (m + 1) * step)
                total_sq = None
                for b in range(2 * groups):
                    prod = jnp.dot(turned[b, rows, :], block, preferred_element_type=jnp.float32)
                    total_sq = prod * prod if total_sq is None else total_sq + prod * prod
                if first:
                    total_sq = total_sq + fisher_ref[rows, at]
                if first + 2 == ways:
                    total_sq = total_sq * scale
                fisher_ref[rows, at] = total_sq

    combine(1)
    bit = 2
    while bit < ways:
        for k in range(2 * bit, ways, 2 * bit):
            combine(k + bit)
            if lowest(k) == 2 * bit:
                send_part(k)
        combine(bit)
        bit *= 2
    grad_ref[...] = acc[0].astype(jnp.bfloat16)
    for k in order:
        for i in range(experts):
            if k or i:
                row_send(k, i).wait_send()
        if k:
            hid_send(k).wait_send()
            part_send(k).wait_send()


def per_device(cotangent, expert_ids, gate_values, hidden, down_weight):
    experts = lax.axis_size("expert")
    ways = lax.axis_size("dp")
    groups, cap, units = hidden.shape[3], hidden.shape[4], hidden.shape[5]
    piece = groups * cap
    slots = experts * piece
    width = down_weight.shape[2]
    tokens, top = expert_ids.shape
    hbm_spec = pl.BlockSpec(memory_space=pltpu.HBM)
    vmem_spec = pl.BlockSpec(memory_space=pltpu.VMEM)
    bf16 = jnp.bfloat16
    operands = (
        expert_ids.T, gate_values.T, cotangent, hidden.reshape(slots, units), down_weight[0],
    )
    fisher, grad = pl.pallas_call(
        functools.partial(route_kernel, experts, ways, groups, cap),
        out_shape=(
            pltpu.VMEM((units, width), jnp.float32),
            pltpu.VMEM((slots, units), bf16),
        ),
        in_specs=[hbm_spec] * 5,
        out_specs=(vmem_spec, vmem_spec),
        scratch_shapes=[
            pltpu.VMEM((top, tokens), jnp.int32),
            pltpu.VMEM((top, tokens), jnp.float32),
            pltpu.VMEM((ways, tokens, width), bf16),
            pltpu.VMEM((units, width), bf16),
            pltpu.VMEM((ways, slots, width), bf16),
            pltpu.VMEM((ways, slots, width), bf16),
            pltpu.VMEM((ways, slots, units), bf16),
            pltpu.VMEM((ways, slots, units), bf16),
            pltpu.VMEM((ways, slots, units), bf16),
            pltpu.VMEM((ways, slots, units), jnp.float32),
            pltpu.VMEM((2 * groups, units, 2 * slots), bf16),
            pltpu.SemaphoreType.DMA((2,)),
            pltpu.SemaphoreType.DMA((ways,)),
            pltpu.SemaphoreType.DMA,
            pltpu.SemaphoreType.DMA,
            pltpu.SemaphoreType.DMA,
            pltpu.SemaphoreType.DMA((ways, experts)),
            pltpu.SemaphoreType.DMA((ways, experts)),
            pltpu.SemaphoreType.DMA((ways,)),
            pltpu.SemaphoreType.DMA((ways,)),
            pltpu.SemaphoreType.DMA((ways,)),
            pltpu.SemaphoreType.DMA((ways,)),
        ],
        compiler_params=pltpu.CompilerParams(
            collective_id=0, has_side_effects=True, vmem_limit_bytes=50 * 2**20
        ),
        name="route",
    )(*(pltpu.with_memory_space_constraint(x, pltpu.HBM) for x in operands))
    return (fisher[None], grad.reshape(hidden.shape))


def solution(mesh):
    in_specs = (
        P(("group", "expert", "dp"), None),
        P(("group", "expert", "dp"), None),
        P(("group", "expert", "dp"), None),
        P(("group", "expert"), "dp", None, None, None, None),
        P("expert", None, "dp"),
    )
    out_specs = (
        P(("group", "expert"), None, "dp"),
        P(("group", "expert"), "dp", None, None, None, None),
    )
    return jax.shard_map(
        per_device, mesh=mesh, in_specs=in_specs, out_specs=out_specs, check_vma=False
    )
```

time: 67.8 us -> 51.5 us (0.76)
  Pallas kernels: 61.6 us -> 47 us
  local copies, waits for them, and re-layouts: 5.24 us -> 3.71 us
    pallas_call x1 -> x0, Pallas kernels: 10.5 us -> none  [per_device(): pl.pallas_call(functools.partial(fisher_kernel, groups, cap, 1.0 / (ways...]
    pallas_call x1, Pallas kernels: 51 us -> 47 us  [per_device(): pl.pallas_call(functools.partial(route_kernel, experts, ways, groups, cap...]
    unnamed x7 -> x2, local copies, waits for them, and re-layouts: 5.24 us -> 3.71 us
where the time goes in v2:
time: 51.5 us; the launch traced here: 51.4 us
  Pallas kernels  47 us (91%)
  local copies, waits for them, and re-layouts  3.71 us (7%)
  between operations  0.64 us (1%)
    pallas_call x1, Pallas kernels, per_device(): pl.pallas_call(functools.partial(route_kernel, experts, ways, groups, cap...  47 us
    unnamed x2, local copies, waits for them, and re-layouts  3.71 us

profile of v2, /device:TPU:0, one launch (start us, length us, event | category | flops | bytes accessed | tf_op | source)
XLA Modules:
  0.0 51.4 jit_solution(15224932182102579091)
XLA Ops:
  0.6 47.0 %route.1 = (f32[1024,1792]{1,0:T(8,128)S(1)}, bf16[64,1024]{1,0:T(8,128)(2,1)S(1)}) custom-call(s32[8,256]{1,0:T(8,128)} %bitcast.10, f32[8,256]{1,0:T(8,128)} %bitcast.11, bf16[256,7168]{1,0:T(8,128)(2,1)} %cot_hbm.1, bf16[64,1024]{1,0:T(8,128)(2,1)} %bitcast.9, bf16[1024,1792]{1,0:T(8,128)(2,1)} %bitcast.8), custom_call_target="tpu_custom_call" | custom-call | tf_op jit(solution)/shard_map/route/pallas_call | solution.py:263
  47.7 3.1 %copy.9 = f32[1,1024,1792]{2,1,0:T(8,128)} copy(f32[1,1024,1792]{2,1,0:T(8,128)S(1)} %bitcast.6) | data formatting | bytes 14680064
  50.7 0.7 %copy.10 = bf16[1,1,4,2,8,1024]{5,4,3,2,1,0:T(8,128)(2,1)} copy(bf16[1,1,4,2,8,1024]{5,4,3,2,1,0:T(8,128)(2,1)S(1)} %bitcast.7) | data formatting | bytes 262144

commit v3 on v2

--- a/solution.py
+++ b/solution.py
@@ -63,7 +63,7 @@
     piece = groups * cap
     units, width = w.shape
     slots = experts * piece
-    order = list(range(ways - 1, -1, -1))
+    order = list(range(ways - 1, 1, -2)) + [1, 0] + list(range(ways - 2, 1, -2))
     peers = [partner(d, k, ways) for k in range(ways)]
 
     def cot_copy(k):
@@ -105,10 +105,14 @@
             device_id=(g, f, peers[lowest(k)]), device_id_type=MESH,
         )
 
-    def part_send(k):
+    parts = 2
+    span = units // parts
+
+    def part_send(k, h):
+        at = pl.ds(h * span, span)
         return pltpu.make_async_remote_copy(
-            src_ref=part_out.at[k], dst_ref=part_in.at[k],
-            send_sem=psend_sem.at[k], recv_sem=precv_sem.at[k],
+            src_ref=part_out.at[k, :, at], dst_ref=part_in.at[k, :, at],
+            send_sem=psend_sem.at[k, h], recv_sem=precv_sem.at[k, h],
             device_id=(g, f, peers[lowest(k)]), device_id_type=MESH,
         )
 
@@ -170,40 +174,43 @@
     lane_half = lax.div(lane, slots)
     scale = 1.0 / (ways * groups)
 
-    def combine(k):
-        part_send(k).wait_recv()
-        acc[k - lowest(k)] += part_in[k].astype(jnp.float32)
-
-    def send_part(k):
-        part_out[k] = acc[k].astype(jnp.bfloat16)
-        part_send(k).start()
-
-    for first in range(0, ways, 2):
-        for k in (first + 1, first):
-            for i in range(experts):
-                if k or i:
-                    row_wait(k, i).wait_recv()
+    def combine(k, h):
+        at = slice(h * span, (h + 1) * span)
+        part_send(k, h).wait_recv()
+        acc[k - lowest(k), :, at] += part_in[k, :, at].astype(jnp.float32)
+
+    def send_part(k, h):
+        at = slice(h * span, (h + 1) * span)
+        part_out[k, :, at] = acc[k, :, at].astype(jnp.bfloat16)
+        part_send(k, h).start()
+
+    def multiply(k):
+        for i in range(experts):
+            if k or i:
+                row_wait(k, i).wait_recv()
+            else:
+                own_copy.wait()
+        for h in range(parts):
+            for n in range(span // tile):
+                at = slice(h * span + n * tile, h * span + (n + 1) * tile)
+                part = lax.dot_general(
+                    cols[k], w[at, :], (((1,), (1,)), ((), ())),
+                    preferred_element_type=jnp.float32,
+                )
+                if k % 2:
+                    part_out[k, :, at] = part.astype(jnp.bfloat16)
                 else:
-                    own_copy.wait()
-
-        pair = cols[first : first + 2].reshape(2 * slots, width)
-        for n in range(units // tile):
-            at = slice(n * tile, (n + 1) * tile)
-            part = lax.dot_general(
-                pair, w[at, :], (((1,), (1,)), ((), ())), preferred_element_type=jnp.float32
-            )
-            acc[first, :, at] = part[:slots]
-            part_out[first + 1, :, at] = part[slots:].astype(jnp.bfloat16)
-        part_send(first + 1).start()
-
-        if first + 2 == ways:
-            for k in range(ways - 2, 0, -2):
-                combine(k + 1)
+                    acc[k, :, at] = part
+            if k % 2:
+                part_send(k, h).start()
+            elif k:
+                combine(k + 1, h)
                 if lowest(k) == 2:
-                    send_part(k)
-
+                    send_part(k, h)
+
+    def add_squares(first):
+        hid_arrive(first)
         hid_arrive(first + 1)
-        hid_arrive(first)
         flat = hidden[first : first + 2].reshape(2 * slots, units).astype(jnp.float32).T
         for h in range(2):
             for j in range(groups):
@@ -227,14 +234,23 @@
                     total_sq = total_sq * scale
                 fisher_ref[rows, at] = total_sq
 
-    combine(1)
+    for k in order:
+        multiply(k)
+        if k == 0:
+            add_squares(0)
+    for first in range(2, ways, 2):
+        add_squares(first)
+
+    for h in range(parts):
+        combine(1, h)
     bit = 2
     while bit < ways:
-        for k in range(2 * bit, ways, 2 * bit):
-            combine(k + bit)
-            if lowest(k) == 2 * bit:
-                send_part(k)
-        combine(bit)
+        for h in range(parts):
+            for k in range(2 * bit, ways, 2 * bit):
+                combine(k + bit, h)
+                if lowest(k) == 2 * bit:
+                    send_part(k, h)
+            combine(bit, h)
         bit *= 2
     grad_ref[...] = acc[0].astype(jnp.bfloat16)
     for k in order:
@@ -243,7 +259,8 @@
                 row_send(k, i).wait_send()
         if k:
             hid_send(k).wait_send()
-            part_send(k).wait_send()
+            for h in range(parts):
+                part_send(k, h).wait_send()
 
 
 def per_device(cotangent, expert_ids, gate_values, hidden, down_weight):
@@ -289,8 +306,8 @@
             pltpu.SemaphoreType.DMA((ways, experts)),
             pltpu.SemaphoreType.DMA((ways,)),
             pltpu.SemaphoreType.DMA((ways,)),
-            pltpu.SemaphoreType.DMA((ways,)),
-            pltpu.SemaphoreType.DMA((ways,)),
+            pltpu.SemaphoreType.DMA((ways, 2)),
+            pltpu.SemaphoreType.DMA((ways, 2)),
         ],
         compiler_params=pltpu.CompilerParams(
             collective_id=0, has_side_effects=True, vmem_limit_bytes=50 * 2**20

time: 51.5 us -> 46.1 us (0.90)
  Pallas kernels: 47 us -> 41.5 us
    pallas_call x1, Pallas kernels: 47 us -> 41.5 us  [per_device(): pl.pallas_call(functools.partial(route_kernel, experts, ways, groups, cap...]
where the time goes in v3:
time: 46.1 us; the launch traced here: 45.9 us
  Pallas kernels  41.5 us (90%)
  local copies, waits for them, and re-layouts  3.71 us (8%)
  between operations  0.64 us (1%)
    pallas_call x1, Pallas kernels, per_device(): pl.pallas_call(functools.partial(route_kernel, experts, ways, groups, cap...  41.5 us
    unnamed x2, local copies, waits for them, and re-layouts  3.71 us

profile of v3, /device:TPU:0, one launch (start us, length us, event | category | flops | bytes accessed | tf_op | source)
XLA Modules:
  0.0 45.9 jit_solution(18271038702008483805)
XLA Ops:
  0.6 41.5 %route.1 = (f32[1024,1792]{1,0:T(8,128)S(1)}, bf16[64,1024]{1,0:T(8,128)(2,1)S(1)}) custom-call(s32[8,256]{1,0:T(8,128)} %bitcast.10, f32[8,256]{1,0:T(8,128)} %bitcast.11, bf16[256,7168]{1,0:T(8,128)(2,1)} %cot_hbm.1, bf16[64,1024]{1,0:T(8,128)(2,1)} %bitcast.9, bf16[1024,1792]{1,0:T(8,128)(2,1)} %bitcast.8), custom_call_target="tpu_custom_call" | custom-call | tf_op jit(solution)/shard_map/route/pallas_call | solution.py:280
  42.2 3.1 %copy.9 = f32[1,1024,1792]{2,1,0:T(8,128)} copy(f32[1,1024,1792]{2,1,0:T(8,128)S(1)} %bitcast.6) | data formatting | bytes 14680064
  45.2 0.7 %copy.10 = bf16[1,1,4,2,8,1024]{5,4,3,2,1,0:T(8,128)(2,1)} copy(bf16[1,1,4,2,8,1024]{5,4,3,2,1,0:T(8,128)(2,1)S(1)} %bitcast.7) | data formatting | bytes 262144
